TPU v7x, 128 devices: a whole 4x4x4 slice. The times are simulated.
128 devices in a mesh: row: 8 (over x_hi, z), col: 16 (over y, x_lo, core).
Axes of the slice: x: 4 (x_hi: 2, x_lo: 2; x = x_hi * 2 + x_lo), y: 4, z: 4, core: 2. Of those that a mesh axis runs over, the one named last changes fastest.
Arguments:
- voxels: bfloat16 [32, 128, 256, 256], P(None, 'row', 'col'), may hold values from -6 to 6
- target: bfloat16 [32, 128, 256, 256], P(None, 'row', 'col'), may hold values from -6 to 6
- weight: bfloat16 [2, 32, 32, 64, 64, 32], P(None, None, None, 'row', 'col'), may hold values from -0.75 to 0.75
Outputs:
- grad_voxels: bfloat16 [32, 128, 256, 256], P(None, 'row', 'col')
- grad_weight: bfloat16 [2, 32, 32, 64, 64, 32], P(None, None, None, 'row', 'col')
All inputs are finite; a program needn't handle non-finite values.
Results may differ from a plain program's by a relative error of at most 0.0011.
Values sent between devices are 32-bit elements; how exact they have to be, the bound alone decides.
No kernel may reach another device: no remote copies, remote signals or barrier semaphores. Data moves between devices by JAX's collectives and lax.ppermute only.
A program may use at most 192 MiB of HBM per device.

v0:
```python
import math

import jax
import jax.numpy as jnp
from jax import lax
from jax.sharding import PartitionSpec as P

X = 128
Y = 256
Z = 256
MX = 32
MY = 64
MZ = 64


HIGHEST_PRECISION = lax.Precision.HIGHEST


def phases(number, length, offset):
    frequency = lax.iota(jnp.int32, number) + offset
    position = lax.iota(jnp.int32, length)
    turns = frequency[:, None] * position[None, :] % length
    return 2.0 * math.pi / length * turns.astype(jnp.float32)


def complex_forward(number, length, offset):
    angle = phases(number, length, offset).T
    cos_table = jnp.cos(angle)
    sin_table = jnp.sin(angle)
    first_rows = jnp.stack([cos_table, -sin_table], 1)
    second_rows = jnp.stack([sin_table, cos_table], 1)
    return jnp.stack([first_rows, second_rows], 0) * length ** (-0.5)


def complex_inverse(number, length, offset):
    angle = phases(number, length, offset)
    cos_table = jnp.cos(angle)
    sin_table = jnp.sin(angle)
    first_rows = jnp.stack([cos_table, sin_table], 1)
    second_rows = jnp.stack([-sin_table, cos_table], 1)
    return jnp.stack([first_rows, second_rows], 0)


def real_forward(number, length):
    angle = phases(number, length, 0).T
    paired = jnp.stack([jnp.cos(angle), -jnp.sin(angle)], 2)
    return paired.reshape(length, 2 * number) * length ** (-0.5)


def real_inverse(number, length):
    angle = phases(number, length, 0)
    paired = jnp.stack([jnp.cos(angle), -jnp.sin(angle)], 1)
    return paired.reshape(2 * number, length)


def per_device(voxels, target, weight):
    ky_local = weight.shape[3]
    kz_local = weight.shape[4]
    z_forward = real_forward(MZ, Z)
    y_forward = complex_forward(MY, Y, -(MY // 2))
    x_forward = complex_forward(MX, X, -(MX // 2))
    x_inverse = complex_inverse(MX, X, -(MX // 2))
    y_inverse = complex_inverse(MY, Y, -(MY // 2))
    z_inverse = real_inverse(MZ, Z)

    def along_y(received):
        shaped = received.reshape(received.shape[:3] + (kz_local, 2))
        lines = jnp.einsum("cxykr,ryRj->cxkjR", shaped, y_forward, precision=HIGHEST_PRECISION)
        return lines.reshape(lines.shape[:3] + (2 * MY,))

    def along_x(received):
        shaped = received.reshape(received.shape[:3] + (ky_local, 2))
        return jnp.einsum("cxkjr,rxRi->Rcjki", shaped, x_forward, precision=HIGHEST_PRECISION)

    def analysis(volume):
        spectra_z = jnp.einsum("cxyz,zq->cxyq", volume, z_forward, precision=HIGHEST_PRECISION)
        middle = along_y(lax.all_to_all(spectra_z, "col", split_axis=3, concat_axis=2, tiled=True))
        return along_x(lax.all_to_all(middle, "row", split_axis=3, concat_axis=1, tiled=True))

    def back_y(received):
        shaped = received.reshape(received.shape[:3] + (MY, 2))
        lines = jnp.einsum("cxkjs,sjRy->cxykR", shaped, y_inverse, precision=HIGHEST_PRECISION)
        return lines.reshape(lines.shape[:3] + (2 * kz_local,))

    def back_z(received):
        return jnp.einsum("cxyq,qz->cxyz", received, z_inverse, precision=HIGHEST_PRECISION)

    def synthesis(spectra):
        lines_x = jnp.einsum("scjki,siRx->cxkjR", spectra, x_inverse, precision=HIGHEST_PRECISION)
        lines_x = lines_x.reshape(lines_x.shape[:3] + (2 * ky_local,))
        middle = back_y(lax.all_to_all(lines_x, "row", split_axis=1, concat_axis=3, tiled=True))
        return back_z(lax.all_to_all(middle, "col", split_axis=2, concat_axis=3, tiled=True))

    weights = weight.astype(jnp.float32)
    spectra = analysis(voxels.astype(jnp.float32))
    real_out = jnp.einsum(
        "cojki,cjki->ojki", weights[0], spectra[0], precision=HIGHEST_PRECISION
    ) - jnp.einsum("cojki,cjki->ojki", weights[1], spectra[1], precision=HIGHEST_PRECISION)
    imag_out = jnp.einsum(
        "cojki,cjki->ojki", weights[0], spectra[1], precision=HIGHEST_PRECISION
    ) + jnp.einsum("cojki,cjki->ojki", weights[1], spectra[0], precision=HIGHEST_PRECISION)
    mixed = jnp.stack([real_out, imag_out])
    factor = math.sqrt(X * Y * Z / (MX * MY * MZ))
    output = synthesis(mixed) * (MX * MY * MZ) ** (-0.5)
    residual = output - target.astype(jnp.float32)
    residual_spectra = analysis(residual)
    cotangent = factor * residual_spectra
    real_grad = spectra[0][:, None] * cotangent[0][None] + spectra[1][:, None] * cotangent[1][None]
    imag_grad = spectra[0][:, None] * cotangent[1][None] - spectra[1][:, None] * cotangent[0][None]
    grad_weight = jnp.stack([real_grad, imag_grad]).astype(jnp.bfloat16)
    real_back = jnp.einsum(
        "cojki,ojki->cjki", weights[0], cotangent[0], precision=HIGHEST_PRECISION
    ) + jnp.einsum("cojki,ojki->cjki", weights[1], cotangent[1], precision=HIGHEST_PRECISION)
    imag_back = jnp.einsum(
        "cojki,ojki->cjki", weights[0], cotangent[1], precision=HIGHEST_PRECISION
    ) - jnp.einsum("cojki,ojki->cjki", weights[1], cotangent[0], precision=HIGHEST_PRECISION)
    back = jnp.stack([real_back, imag_back])
    grad_voxels = (synthesis(back) * (X * Y * Z) ** (-0.5)).astype(jnp.bfloat16)
    return (grad_voxels, grad_weight)


def solution(mesh):
    placed = (
        P(None, "row", "col", None),
        P(None, "row", "col", None),
        P(None, None, None, "row", "col", None),
    )
    return jax.shard_map(
        per_device,
        mesh=mesh,
        in_specs=placed,
        out_specs=(P(None, "row", "col", None), P(None, None, None, "row", "col", None)),
        check_vma=False,
    )
```

profile of v0, /device:TPU:1, one launch (start us, length us, event | category | flops | bytes accessed | tf_op | source)
XLA Modules:
  0.0 866.4 jit_solution(12566348114881490496)
XLA Ops:
  10.3 14.3 %copy.199 = f32[32,16,16,128]{0,2,1,3:T(8,128)} copy(f32[32,16,16,128]{3,0,2,1:T(8,128)} %fusion.15) | data formatting | bytes 8388608 | tf_op jit(solution)/shard_map/cxyz,zq->cxyq/dot_general | solution.py:76
  24.6 16.0 %reshape.747 = f32[16,1,65536]{2,1,0:T(1,128)} reshape(f32[128,16,16,32]{3,2,1,0:T(8,128)} %bitcast.263) | data formatting | bytes 8388608
  48.6 49.1 %all-to-all-done = f32[16,1,65536]{2,1,0:T(1,128)} async-done(((f32[16,1,65536]{2,1,0:T(1,128)}), f32[16,1,65536]{2,1,0:T(1,128)}, u32[]{:S(2)}, u32[]{:S(2)}) %all-to-all-start) | async-done | bytes 4194336 | tf_op jit(solution)/shard_map/all_to_all | solution.py:77
  112.1 15.4 %reshape.748 = f32[128,16,16,32]{3,2,1,0:T(8,128)} reshape(f32[16,65536]{1,0:T(8,128)} %reduce.16) | data formatting | bytes 8388608
  134.7 27.1 %convolution_bitcast_fusion.3 = f32[32,16,4,64,2]{3,0,2,1,4:T(8,128)S(1)} fusion(f32[32,16,256,4,2,1]{0,2,4,3,1,5:T(8,128)S(1)} %bitcast.274, f32[1,256,2,64]{1,3,0,2:T(8,128)S(1)} %get-tuple-element.27, f32[1,256,2,64]{1,3,0,2:T(8,128)S(1)} %get-tuple-element.26), kind=kOutput, calls=%fused_computation.35 | convolution fusion | flops 1610743808 | bytes 5505024 | tf_op jit(solution)/shard_map/cxykr,ryRj->cxkjR/dot_general | solution.py:68
  207.1 23.6 %fusion = (f32[8,4,32,32]{2,1,0,3:T(4,128)S(1)}, f32[8,4,32,32]{2,1,0,3:T(4,128)S(1)}, f32[8,4,32,32]{2,1,0,3:T(4,128)S(1)}, f32[8,4,32,32]{2,1,0,3:T(4,128)S(1)}) fusion(f32[8,4,32,32]{2,1,0,3:T(4,128)S(1)} %copy.338, bf16[2,32,32,8,4,32]{5,4,3,2,1,0:T(4,128)(2,1)} %param.5, f32[8,4,32,32]{2,1,0,3:T(4,128)S(1)} %copy.339), kind=kLoop, calls=%fused_computation.8 | loop fusion | flops 10354688 | bytes 4980736
  248.8 14.0 %all-to-all-done.2 = f32[8,1,32768]{2,1,0:T(1,128)S(1)} async-done(((f32[8,1,32768]{2,1,0:T(1,128)}), f32[8,1,32768]{2,1,0:T(1,128)S(1)}, u32[]{:S(2)}, u32[]{:S(2)}) %all-to-all-start.2) | async-done | bytes 1048608 | tf_op jit(solution)/shard_map/all_to_all | solution.py:91
  287.2 15.0 %copy.213 = f32[32,16,256,8]{0,3,1,2:T(8,128)} copy(f32[32,16,256,8]{2,1,3,0:T(8,128)} %bitcast.277) | data formatting | bytes 8388608 | tf_op jit(solution)/shard_map/reshape | solution.py:83
  302.1 16.0 %reshape.753 = f32[16,1,65536]{2,1,0:T(1,128)} reshape(f32[256,16,8,32]{3,2,1,0:T(8,128)} %bitcast.264) | data formatting | bytes 8388608
  325.8 49.1 %all-to-all-done.3 = f32[16,1,65536]{2,1,0:T(1,128)} async-done(((f32[16,1,65536]{2,1,0:T(1,128)}), f32[16,1,65536]{2,1,0:T(1,128)}, u32[]{:S(2)}, u32[]{:S(2)}) %all-to-all-start.3) | async-done | bytes 4194336 | tf_op jit(solution)/shard_map/all_to_all | solution.py:92
  388.6 15.4 %reshape.754 = f32[256,16,8,32]{3,2,1,0:T(8,128)} reshape(f32[16,65536]{1,0:T(8,128)} %reduce.19) | data formatting | bytes 8388608
  444.9 14.5 %copy.219 = f32[32,16,16,128]{0,2,1,3:T(8,128)} copy(f32[32,16,16,128]{3,2,1,0:T(8,128)} %fusion.8) | data formatting | bytes 8388608 | tf_op jit(solution)/shard_map/cxyz,zq->cxyq/dot_general | solution.py:76
  459.4 16.0 %reshape.755 = f32[16,1,65536]{2,1,0:T(1,128)} reshape(f32[128,16,16,32]{3,2,1,0:T(8,128)} %bitcast.265) | data formatting | bytes 8388608
  475.3 54.4 %all_to_all.126 = f32[16,1,65536]{2,1,0:T(1,128)} all-to-all(f32[16,1,65536]{2,1,0:T(1,128)} %reshape.755), channel_id=1, replica_groups=mesh['row'=8,'col'=16] {'col'}, dimensions={0} | all-to-all | bytes 8388608 | tf_op jit(solution)/shard_map/all_to_all | solution.py:77
  543.6 15.4 %reshape.756 = f32[128,16,16,32]{3,2,1,0:T(8,128)} reshape(f32[16,65536]{1,0:T(8,128)} %reduce.20) | data formatting | bytes 8388608
  566.1 27.3 %convolution_bitcast_fusion.2 = f32[32,16,4,64,2]{3,0,2,1,4:T(8,128)S(1)} fusion(f32[32,16,256,4,2,1]{0,2,4,3,1,5:T(8,128)S(1)} %bitcast.273, f32[1,256,2,64]{1,3,0,2:T(8,128)S(1)} %get-tuple-element.27, f32[1,256,2,64]{1,3,0,2:T(8,128)S(1)} %get-tuple-element.26), kind=kOutput, calls=%fused_computation.34 | convolution fusion | flops 1610743808 | bytes 5505024 | tf_op jit(solution)/shard_map/cxykr,ryRj->cxkjR/dot_general | solution.py:68
  601.9 18.7 %all_to_all.127 = f32[8,1,32768]{2,1,0:T(1,128)S(1)} all-to-all(f32[8,1,32768]{2,1,0:T(1,128)S(1)} %reshape.757), channel_id=1, replica_groups=mesh['row'=8,'col'=16] {'row'}, dimensions={0} | all-to-all | bytes 2097152 | tf_op jit(solution)/shard_map/all_to_all | solution.py:78
  634.0 27.5 %fusion.4 = (f32[8,4,32,32]{2,1,0,3:T(4,128)S(1)}, f32[8,4,32,32]{2,1,0,3:T(4,128)S(1)}, f32[8,4,32,32]{2,1,0,3:T(4,128)S(1)}, f32[8,4,32,32]{2,1,0,3:T(4,128)S(1)}) fusion(f32[8,4,32,32]{2,1,0,3:T(4,128)S(1)} %copy.340, bf16[2,32,32,8,4,32]{5,4,3,2,1,0:T(4,128)(2,1)} %param.5, f32[8,4,32,32]{2,1,0,3:T(4,128)S(1)} %copy.341), kind=kLoop, calls=%fused_computation.12 | loop fusion | flops 10354688 | bytes 4980736
  672.2 17.9 %all_to_all.128 = f32[8,1,32768]{2,1,0:T(1,128)S(1)} all-to-all(f32[8,1,32768]{2,1,0:T(1,128)S(1)} %reshape.759), channel_id=1, replica_groups=mesh['row'=8,'col'=16] {'row'}, dimensions={0} | all-to-all | bytes 2097152 | tf_op jit(solution)/shard_map/all_to_all | solution.py:91
  714.6 15.0 %copy.233 = f32[32,16,256,8]{0,3,1,2:T(8,128)} copy(f32[32,16,256,8]{2,1,3,0:T(8,128)} %bitcast.280) | data formatting | bytes 8388608 | tf_op jit(solution)/shard_map/reshape | solution.py:83
  729.6 16.0 %reshape.761 = f32[16,1,65536]{2,1,0:T(1,128)} reshape(f32[256,16,8,32]{3,2,1,0:T(8,128)} %bitcast.266) | data formatting | bytes 8388608
  766.0 15.4 %pad_maximum_fusion = bf16[2,32,32,8,4,32]{5,4,3,2,1,0:T(4,128)(2,1)} fusion(bf16[1,32,32,8,4,32]{5,4,3,2,1,0:T(4,128)(2,1)S(1)} %get-tuple-element.15, bf16[1,32,32,8,4,32]{5,4,3,2,1,0:T(4,128)(2,1)S(1)} %get-tuple-element.14), kind=kLoop, calls=%fused_computation.16 | loop fusion | flops 2097152 | bytes 8388608 | tf_op jit(solution)/shard_map/stack | solution.py:110
  781.3 22.4 %all-to-all-done.7 = f32[16,1,65536]{2,1,0:T(1,128)} async-done(((f32[16,1,65536]{2,1,0:T(1,128)}), f32[16,1,65536]{2,1,0:T(1,128)}, u32[]{:S(2)}, u32[]{:S(2)}) %all-to-all-start.7) | async-done | bytes 4194336 | tf_op jit(solution)/shard_map/all_to_all | solution.py:92
  817.6 15.1 %reshape.762 = f32[256,16,8,32]{3,2,1,0:T(8,128)} reshape(f32[16,65536]{1,0:T(8,128)} %reduce.23) | data formatting | bytes 8388608
  (100 shorter events, 334.2 us)
Async XLA Ops:
  40.6 57.2 %all-to-all-start = ((f32[16,1,65536]{2,1,0:T(1,128)}), f32[16,1,65536]{2,1,0:T(1,128)}, u32[]{:S(2)}, u32[]{:S(2)}) async-start(f32[16,1,65536]{2,1,0:T(1,128)} %reshape.747), calls=%async_computation | async-start | bytes 8388608 | tf_op jit(solution)/shard_map/all_to_all | solution.py:77
  171.1 21.6 %all-to-all-start.1 = ((f32[8,1,32768]{2,1,0:T(1,128)}), f32[8,1,32768]{2,1,0:T(1,128)S(1)}, u32[]{:S(2)}, u32[]{:S(2)}) async-start(f32[8,1,32768]{2,1,0:T(1,128)} %reshape.749), calls=%async_computation.1 | async-start | bytes 2097152 | tf_op jit(solution)/shard_map/all_to_all | solution.py:78
  178.9 53.0 %copy-start.3 = (f32[1,32,2,128]{3,1,0,2:T(8,128)}, f32[1,32,2,128]{3,1,0,2:T(8,128)S(1)}, u32[]{:S(2)}) copy-start(f32[1,32,2,128]{3,1,0,2:T(8,128)S(1)} %get-tuple-element.28) | copy-start | bytes 98308
  178.9 53.0 %copy-start.5 = (f32[1,32,2,128]{3,1,0,2:T(8,128)}, f32[1,32,2,128]{3,1,0,2:T(8,128)S(1)}, u32[]{:S(2)}) copy-start(f32[1,32,2,128]{3,1,0,2:T(8,128)S(1)} %get-tuple-element.29) | copy-start | bytes 98308
  242.3 20.5 %all-to-all-start.2 = ((f32[8,1,32768]{2,1,0:T(1,128)}), f32[8,1,32768]{2,1,0:T(1,128)S(1)}, u32[]{:S(2)}, u32[]{:S(2)}) async-start(f32[8,1,32768]{2,1,0:T(1,128)} %reshape.751), calls=%async_computation.2 | async-start | bytes 2097152 | tf_op jit(solution)/shard_map/all_to_all | solution.py:91
  318.1 56.7 %all-to-all-start.3 = ((f32[16,1,65536]{2,1,0:T(1,128)}), f32[16,1,65536]{2,1,0:T(1,128)}, u32[]{:S(2)}, u32[]{:S(2)}) async-start(f32[16,1,65536]{2,1,0:T(1,128)} %reshape.753), calls=%async_computation.3 | async-start | bytes 8388608 | tf_op jit(solution)/shard_map/all_to_all | solution.py:92
  427.6 8.8 %copy-start = (bf16[32,16,16,256]{3,2,1,0:T(8,128)(2,1)S(1)}, bf16[32,16,16,256]{3,2,1,0:T(8,128)(2,1)}, u32[]{:S(2)}) copy-start(bf16[32,16,16,256]{3,2,1,0:T(8,128)(2,1)} %param.4) | copy-start | bytes 12582916
  634.0 28.7 %copy-start.4 = (f32[1,32,2,128]{3,1,0,2:T(8,128)S(1)}, f32[1,32,2,128]{3,1,0,2:T(8,128)}, u32[]{:S(2)}) copy-start(f32[1,32,2,128]{3,1,0,2:T(8,128)} %copy-done.3) | copy-start | bytes 98308
  634.0 28.7 %copy-start.6 = (f32[1,32,2,128]{3,1,0,2:T(8,128)S(1)}, f32[1,32,2,128]{3,1,0,2:T(8,128)}, u32[]{:S(2)}) copy-start(f32[1,32,2,128]{3,1,0,2:T(8,128)} %copy-done.5) | copy-start | bytes 98308
  745.6 8.6 copy-start.2
  745.6 9.1 %copy-start.1 = (f32[32,8,4,32]{0,3,1,2:T(8,128)S(1)}, f32[32,8,4,32]{0,3,1,2:T(8,128)}, u32[]{:S(2)}) copy-start(f32[32,8,4,32]{0,3,1,2:T(8,128)} %get-tuple-element.19) | copy-start | bytes 393220
  745.6 58.2 %all-to-all-start.7 = ((f32[16,1,65536]{2,1,0:T(1,128)}), f32[16,1,65536]{2,1,0:T(1,128)}, u32[]{:S(2)}, u32[]{:S(2)}) async-start(f32[16,1,65536]{2,1,0:T(1,128)} %reshape.761), calls=%async_computation.7 | async-start | bytes 8388608 | tf_op jit(solution)/shard_map/all_to_all | solution.py:92
where the time goes:
time: 875 us; the launch traced here: 866 us
  local copies, waits for them, and re-layouts  336 us (38%)
  other arithmetic  148 us (17%)
  waiting for transfers between devices  148 us (17%)
  matrix products  105 us (12%)
  blocking collectives  91 us (10%)
  starting transfers between devices  37.1 us (4%)
    unnamed x34, local copies, waits for them, and re-layouts  159 us
    all_to_all x2, waiting for transfers between devices, synthesis(): lax.all_to_all(middle, 'col', split_axis=2, concat_axis=3, tiled=True)  71.5 us
    all_to_all x1, blocking collectives, analysis(): lax.all_to_all(spectra_z, 'col', split_axis=3, concat_axis=2, tiled=True)  54.4 us
    dot_general x2, matrix products, along_y(): jnp.einsum('cxykr,ryRj->cxkjR', shaped, y_forward, precision=HIGHEST_PREC...  54.4 us
    unnamed x2, other arithmetic  51.2 us
    all_to_all x1, waiting for transfers between devices, analysis(): lax.all_to_all(spectra_z, 'col', split_axis=3, concat_axis=2, tiled=True)  49.1 us
    all_to_all x4, local copies, waits for them, and re-layouts, synthesis(): lax.all_to_all(middle, 'col', split_axis=2, concat_axis=3, tiled=True)  47.1 us
    reshape x2, local copies, waits for them, and re-layouts, back_y(): return lines.reshape(lines.shape[:3] + (2 * kz_local,))  30 us
  transfers between devices with their start and end apart: 5, of which 5 were waited for; matrix products, arithmetic and copies ran while one was open for 3% of the time, Pallas kernels for 0%

commit v1 on v0

--- a/solution.py
+++ b/solution.py
@@ -91,6 +91,15 @@
         middle = back_y(lax.all_to_all(lines_x, "row", split_axis=1, concat_axis=3, tiled=True))
         return back_z(lax.all_to_all(middle, "col", split_axis=2, concat_axis=3, tiled=True))
 
+    def hermitian_partner(modes):
+        plane = modes[:, :, :, 0, :]
+        rows = lax.axis_size("row")
+        same = lax.ppermute(plane, "row", [(b, rows - 1 - b) for b in range(rows)])
+        edge = lax.ppermute(plane[:, :, :1], "row", [(b, rows - b) for b in range(1, rows)])
+        by_ky = jnp.concatenate([edge, same[:, :, :0:-1]], 2)
+        by_kx = jnp.concatenate([jnp.zeros_like(by_ky[..., :1]), by_ky[..., :0:-1]], 3)
+        return (by_kx * jnp.array([1.0, -1.0], jnp.float32)[:, None, None, None])[:, :, :, None, :]
+
     weights = weight.astype(jnp.float32)
     spectra = analysis(voxels.astype(jnp.float32))
     real_out = jnp.einsum(
@@ -100,11 +109,12 @@
         "cojki,cjki->ojki", weights[0], spectra[1], precision=HIGHEST_PRECISION
     ) + jnp.einsum("cojki,cjki->ojki", weights[1], spectra[0], precision=HIGHEST_PRECISION)
     mixed = jnp.stack([real_out, imag_out])
+    scale = 0.5 * math.sqrt(X * Y * Z / (MX * MY * MZ))
     factor = math.sqrt(X * Y * Z / (MX * MY * MZ))
-    output = synthesis(mixed) * (MX * MY * MZ) ** (-0.5)
-    residual = output - target.astype(jnp.float32)
-    residual_spectra = analysis(residual)
-    cotangent = factor * residual_spectra
+    mirrored = hermitian_partner(mixed)
+    first_plane = (lax.axis_index("col") == 0) & (jnp.arange(kz_local) == 0)
+    output_spectra = scale * (mixed + jnp.where(first_plane[:, None], mirrored, 0.0))
+    cotangent = factor * (output_spectra - analysis(target.astype(jnp.float32)))
     real_grad = spectra[0][:, None] * cotangent[0][None] + spectra[1][:, None] * cotangent[1][None]
     imag_grad = spectra[0][:, None] * cotangent[1][None] - spectra[1][:, None] * cotangent[0][None]
     grad_weight = jnp.stack([real_grad, imag_grad]).astype(jnp.bfloat16)

time: 875 us -> 629 us (0.72)
  waiting for transfers between devices: 148 us -> 44.5 us
  blocking collectives: 91 us -> 0 us
  local copies, waits for them, and re-layouts: 336 us -> 292 us
  other arithmetic: 148 us -> 110 us
  matrix products: 105 us -> 122 us
  starting transfers between devices: 37.1 us -> 49.8 us
    all_to_all x3 -> x0, blocking collectives: 91 us -> none  [the longest x1 54.4 us: analysis(): lax.all_to_all(spectra_z, 'col', split_axis=3, concat_axis=2, tiled=True)]
    all_to_all x2 -> x1, waiting for transfers between devices: 71.5 us -> 21.9 us  [synthesis(): lax.all_to_all(middle, 'col', split_axis=2, concat_axis=3, tiled=True)]
    squeeze x0 -> x3, local copies, waits for them, and re-layouts: none -> 47.2 us  [the longest x2 31.8 us: per_device(): weights[0]]
    all_to_all x1 -> x2, waiting for transfers between devices: 49.1 us -> 10.1 us  [analysis(): lax.all_to_all(spectra_z, 'col', split_axis=3, concat_axis=2, tiled=True)]
    unnamed x34, local copies, waits for them, and re-layouts: 159 us -> 121 us
    dot_general x0 -> x4, matrix products: none -> 28.2 us  [the longest x1 7.2 us: per_device(): jnp.einsum('cojki,cjki->ojki', weights[0], spectra[0], precision=HIGHEST_...]
    unnamed x2 -> x3, other arithmetic: 51.2 us -> 27.3 us
    all_to_all x4 -> x2, local copies, waits for them, and re-layouts: 47.1 us -> 23.6 us  [synthesis(): lax.all_to_all(middle, 'col', split_axis=2, concat_axis=3, tiled=True)]
  transfers between devices with their start and end apart: 5 -> 8, of which waited for: 5 -> 3; matrix products, arithmetic and copies ran while one was open for 3% -> 51% of each run, Pallas kernels for 0% -> 0%
where the time goes in v1:
time: 629 us; the launch traced here: 620 us
  local copies, waits for them, and re-layouts  292 us (46%)
  matrix products  122 us (19%)
  other arithmetic  110 us (17%)
  starting transfers between devices  49.8 us (8%)
  waiting for transfers between devices  44.5 us (7%)
    unnamed x34, local copies, waits for them, and re-layouts  121 us
    dot_general x2, matrix products, along_y(): jnp.einsum('cxykr,ryRj->cxkjR', shaped, y_forward, precision=HIGHEST_PREC...  54.4 us
    squeeze x2, local copies, waits for them, and re-layouts, per_device(): weights[0]  31.8 us
    dot_general x2, local copies, waits for them, and re-layouts, analysis(): jnp.einsum('cxyz,zq->cxyq', volume, z_forward, precision=HIGHEST_PRECISION)  28.7 us
    all_to_all x2, other arithmetic, analysis(): lax.all_to_all(spectra_z, 'col', split_axis=3, concat_axis=2, tiled=True)  27.5 us
    unnamed x3, other arithmetic  27.3 us
    all_to_all x2, local copies, waits for them, and re-layouts, synthesis(): lax.all_to_all(middle, 'col', split_axis=2, concat_axis=3, tiled=True)  23.6 us
    all_to_all x1, waiting for transfers between devices, synthesis(): lax.all_to_all(middle, 'col', split_axis=2, concat_axis=3, tiled=True)  21.9 us
  transfers between devices with their start and end apart: 8, of which 3 were waited for; matrix products, arithmetic and copies ran while one was open for 51% of the time, Pallas kernels for 0%

profile of v1, /device:TPU:1, one launch (start us, length us, event | category | flops | bytes accessed | tf_op | source)
XLA Modules:
  0.0 619.6 jit_solution(2401267655003462261)
XLA Ops:
  10.3 14.3 %copy.174 = f32[32,16,16,128]{0,2,1,3:T(8,128)} copy(f32[32,16,16,128]{3,0,2,1:T(8,128)} %fusion.8) | data formatting | bytes 8388608 | tf_op jit(solution)/shard_map/cxyz,zq->cxyq/dot_general | solution.py:76
  24.6 16.0 %reshape.734 = f32[16,1,65536]{2,1,0:T(1,128)} reshape(f32[128,16,16,32]{3,2,1,0:T(8,128)} %bitcast.230) | data formatting | bytes 8388608
  57.0 14.3 %copy.185 = f32[32,16,16,128]{0,2,1,3:T(8,128)} copy(f32[32,16,16,128]{3,0,2,1:T(8,128)} %fusion.11) | data formatting | bytes 8388608 | tf_op jit(solution)/shard_map/cxyz,zq->cxyq/dot_general | solution.py:76
  71.3 16.0 %reshape.730 = f32[16,1,65536]{2,1,0:T(1,128)} reshape(f32[128,16,16,32]{3,2,1,0:T(8,128)} %bitcast.231) | data formatting | bytes 8388608
  87.3 10.1 %all-to-all-done = f32[16,1,65536]{2,1,0:T(1,128)} async-done(((f32[16,1,65536]{2,1,0:T(1,128)}), f32[16,1,65536]{2,1,0:T(1,128)}, u32[]{:S(2)}, u32[]{:S(2)}) %all-to-all-start) | async-done | bytes 4194336 | tf_op jit(solution)/shard_map/all_to_all | solution.py:77
  102.9 16.3 %slice_bitcast_fusion.1 = (bf16[32,32,8,4,32]{4,3,2,1,0:T(4,128)(2,1)}, bf16[32,32,8,4,32]{4,3,2,1,0:T(4,128)(2,1)}) fusion(bf16[2,32,32,8,4,32]{5,4,3,2,1,0:T(4,128)(2,1)} %param.6), kind=kLoop, calls=%fused_computation.14 | loop fusion | bytes 8388608 | tf_op jit(solution)/shard_map/squeeze | solution.py:106
  119.2 15.5 %copy.216 = bf16[32,32,8,4,32]{1,0,4,3,2:T(8,128)(2,1)} copy(bf16[32,32,8,4,32]{4,3,2,1,0:T(4,128)(2,1)} %get-tuple-element.8) | data formatting | bytes 4194304 | tf_op jit(solution)/shard_map/squeeze | solution.py:106
  134.7 15.4 %copy.219 = bf16[32,32,8,4,32]{1,0,4,3,2:T(8,128)(2,1)} copy(bf16[32,32,8,4,32]{4,3,2,1,0:T(4,128)(2,1)} %get-tuple-element.9) | data formatting | bytes 4194304 | tf_op jit(solution)/shard_map/squeeze | solution.py:107
  152.2 13.7 %reduce.10 = f32[16,65536]{1,0:T(8,128)} reduce(f32[16,1,65536]{2,1,0:T(1,128)} %all-to-all-done, f32[]{:T(128)} %broadcast.915), dimensions={1}, to_apply=%all_to_all.68.reduce_sub_computation | reduce | bytes 8388612 | tf_op jit(solution)/shard_map/all_to_all | solution.py:77
  165.9 15.4 %reshape.735 = f32[128,16,16,32]{3,2,1,0:T(8,128)} reshape(f32[16,65536]{1,0:T(8,128)} %reduce.10) | data formatting | bytes 8388608
  188.7 27.1 %convolution_bitcast_fusion.2 = f32[32,16,4,64,2]{3,0,2,1,4:T(8,128)S(1)} fusion(f32[32,16,256,4,2,1]{0,2,4,3,1,5:T(8,128)S(1)} %bitcast.238, f32[1,256,2,64]{1,3,0,2:T(8,128)S(1)} %get-tuple-element.23, f32[1,256,2,64]{1,3,0,2:T(8,128)S(1)} %get-tuple-element.22), kind=kOutput, calls=%fused_computation.24 | convolution fusion | flops 1610743808 | bytes 5505024 | tf_op jit(solution)/shard_map/cxykr,ryRj->cxkjR/dot_general | solution.py:68
  233.1 13.8 %reduce.8 = f32[16,65536]{1,0:T(8,128)} reduce(f32[16,1,65536]{2,1,0:T(1,128)} %all-to-all-done.2, f32[]{:T(128)} %broadcast.915), dimensions={1}, to_apply=%all_to_all.74.reduce_sub_computation | reduce | bytes 8388612 | tf_op jit(solution)/shard_map/all_to_all | solution.py:77
  246.9 15.4 %reshape.731 = f32[128,16,16,32]{3,2,1,0:T(8,128)} reshape(f32[16,65536]{1,0:T(8,128)} %reduce.8) | data formatting | bytes 8388608
  269.5 27.3 %convolution_bitcast_fusion.1 = f32[32,16,4,64,2]{3,0,2,1,4:T(8,128)S(1)} fusion(f32[32,16,256,4,2,1]{0,2,4,3,1,5:T(8,128)S(1)} %bitcast.237, f32[1,256,2,64]{1,3,0,2:T(8,128)S(1)} %get-tuple-element.23, f32[1,256,2,64]{1,3,0,2:T(8,128)S(1)} %get-tuple-element.22), kind=kOutput, calls=%fused_computation.23 | convolution fusion | flops 1610743808 | bytes 5505024 | tf_op jit(solution)/shard_map/cxykr,ryRj->cxkjR/dot_general | solution.py:68
  383.6 27.3 %fusion = (f32[8,4,32,32]{2,1,0,3:T(4,128)S(1)}, f32[8,4,32,32]{2,1,0,3:T(4,128)S(1)}, f32[8,4,32,32]{2,1,0,3:T(4,128)S(1)}, f32[8,4,32,32]{2,1,0,3:T(4,128)S(1)}) fusion(f32[8,4,32,32]{2,1,0,3:T(4,128)S(1)} %copy.278, bf16[2,32,32,8,4,32]{5,4,3,2,1,0:T(4,128)(2,1)} %param.6, f32[8,4,32,32]{2,1,0,3:T(4,128)S(1)} %copy.279), kind=kLoop, calls=%fused_computation.4 | loop fusion | flops 10354688 | bytes 4980736
  429.8 12.6 %all-to-all-done.4 = f32[8,1,32768]{2,1,0:T(1,128)S(1)} async-done(((f32[8,1,32768]{2,1,0:T(1,128)}), f32[8,1,32768]{2,1,0:T(1,128)S(1)}, u32[]{:S(2)}, u32[]{:S(2)}) %all-to-all-start.4) | async-done | bytes 1048608 | tf_op jit(solution)/shard_map/all_to_all | solution.py:91
  466.7 15.0 %copy.199 = f32[32,16,256,8]{0,3,1,2:T(8,128)} copy(f32[32,16,256,8]{2,1,3,0:T(8,128)} %bitcast.242) | data formatting | bytes 8388608 | tf_op jit(solution)/shard_map/reshape | solution.py:83
  481.7 16.0 %reshape.740 = f32[16,1,65536]{2,1,0:T(1,128)} reshape(f32[256,16,8,32]{3,2,1,0:T(8,128)} %bitcast.232) | data formatting | bytes 8388608
  519.3 15.4 %pad_maximum_fusion = bf16[2,32,32,8,4,32]{5,4,3,2,1,0:T(4,128)(2,1)} fusion(bf16[1,32,32,8,4,32]{5,4,3,2,1,0:T(4,128)(2,1)S(1)} %get-tuple-element.11, bf16[1,32,32,8,4,32]{5,4,3,2,1,0:T(4,128)(2,1)S(1)} %get-tuple-element.10), kind=kLoop, calls=%fused_computation.8 | loop fusion | flops 2097152 | bytes 8388608 | tf_op jit(solution)/shard_map/stack | solution.py:120
  534.7 21.9 %all-to-all-done.5 = f32[16,1,65536]{2,1,0:T(1,128)} async-done(((f32[16,1,65536]{2,1,0:T(1,128)}), f32[16,1,65536]{2,1,0:T(1,128)}, u32[]{:S(2)}, u32[]{:S(2)}) %all-to-all-start.5) | async-done | bytes 4194336 | tf_op jit(solution)/shard_map/all_to_all | solution.py:92
  556.6 13.8 %reduce.13 = f32[16,65536]{1,0:T(8,128)} reduce(f32[16,1,65536]{2,1,0:T(1,128)} %all-to-all-done.5, f32[]{:T(128)} %broadcast.915), dimensions={1}, to_apply=%all_to_all.83.reduce_sub_computation | reduce | bytes 8388612 | tf_op jit(solution)/shard_map/all_to_all | solution.py:92
  570.4 15.1 %reshape.741 = f32[256,16,8,32]{3,2,1,0:T(8,128)} reshape(f32[16,65536]{1,0:T(8,128)} %reduce.13) | data formatting | bytes 8388608
  585.5 11.9 %copy.311 = f32[32,16,16,16,8]{0,4,3,2,1:T(8,128)} copy(f32[32,16,16,16,8]{0,4,1,2,3:T(8,128)} %bitcast.235) | data formatting | bytes 8388608 | tf_op jit(solution)/shard_map/all_to_all | solution.py:92
  597.3 11.8 %copy.203 = f32[32,16,16,128]{3,2,1,0:T(8,128)} copy(f32[32,16,16,128]{0,3,2,1:T(8,128)} %bitcast.236) | data formatting | bytes 8388608 | tf_op jit(solution)/shard_map/all_to_all | solution.py:92
  (106 shorter events, 226.7 us)
Async XLA Ops:
  40.6 56.8 %all-to-all-start = ((f32[16,1,65536]{2,1,0:T(1,128)}), f32[16,1,65536]{2,1,0:T(1,128)}, u32[]{:S(2)}, u32[]{:S(2)}) async-start(f32[16,1,65536]{2,1,0:T(1,128)} %reshape.734), calls=%async_computation | async-start | bytes 8388608 | tf_op jit(solution)/shard_map/all_to_all | solution.py:77
  97.4 127.7 %all-to-all-start.2 = ((f32[16,1,65536]{2,1,0:T(1,128)}), f32[16,1,65536]{2,1,0:T(1,128)}, u32[]{:S(2)}, u32[]{:S(2)}) async-start(f32[16,1,65536]{2,1,0:T(1,128)} %reshape.730), calls=%async_computation.2 | async-start | bytes 8388608 | tf_op jit(solution)/shard_map/all_to_all | solution.py:77
  150.1 0.5 copy-start.3
  225.1 81.0 %all-to-all-start.1 = ((f32[8,1,32768]{2,1,0:T(1,128)}), f32[8,1,32768]{2,1,0:T(1,128)S(1)}, u32[]{:S(2)}, u32[]{:S(2)}) async-start(f32[8,1,32768]{2,1,0:T(1,128)} %reshape.736), calls=%async_computation.1 | async-start | bytes 2097152 | tf_op jit(solution)/shard_map/all_to_all | solution.py:78
  306.1 1.0 copy-start
  307.1 57.2 %all-to-all-start.3 = ((f32[8,1,32768]{2,1,0:T(1,128)}), f32[8,1,32768]{2,1,0:T(1,128)S(1)}, u32[]{:S(2)}, u32[]{:S(2)}) async-start(f32[8,1,32768]{2,1,0:T(1,128)} %reshape.732), calls=%async_computation.3 | async-start | bytes 2097152 | tf_op jit(solution)/shard_map/all_to_all | solution.py:78
  321.8 6.8 %slice-start.2 = ((s8[8388608]{0:T(1024)(128)(4,1)}), s8[4194304]{0:T(1024)(128)(4,1)S(1)}, s32[]{:S(2)}) async-start(s8[8388608]{0:T(1024)(128)(4,1)} %bitcast.251), calls=%async_computation.8 | async-start | bytes 8388608
  324.7 3.8 slice-start.3
  328.5 14.2 %slice-start = ((s8[8388608]{0:T(1024)(128)(4,1)}), s8[4194304]{0:T(1024)(128)(4,1)S(1)}, s32[]{:S(2)}) async-start(s8[8388608]{0:T(1024)(128)(4,1)} %bitcast.249), calls=%async_computation.6 | async-start | bytes 8388608
  335.5 7.2 %slice-start.1 = ((s8[8388608]{0:T(1024)(128)(4,1)}), s8[4194304]{0:T(1024)(128)(4,1)S(1)}, s32[]{:S(2)}) async-start(s8[8388608]{0:T(1024)(128)(4,1)} %bitcast.249), calls=%async_computation.7 | async-start | bytes 8388608
  357.6 18.1 %collective-permute-start.1 = (f32[2,32,8,32]{1,3,2,0:T(8,128)S(1)}, f32[2,32,8,32]{1,3,2,0:T(8,128)}, u32[]{:S(2)}, u32[]{:S(2)}) collective-permute-start(f32[2,32,8,32]{1,3,2,0:T(8,128)S(1)} %fusion.34), channel_id=1, source_target_pairs={{0,112},{16,96},{32,80},{48,64},{64,48},{80,32},{96,16},{112,0},{1... | collective-permute-start | bytes 196616 | tf_op jit(solution)/shard_map/ppermute | solution.py:97
  362.7 14.1 %collective-permute-start = (f32[2,32,1,32]{1,3,2,0:T(8,128)}, f32[2,32,1,32]{1,3,2,0:T(8,128)}, u32[]{:S(2)}, u32[]{:S(2)}) collective-permute-start(f32[2,32,1,32]{1,3,2,0:T(8,128)} %slice.62), channel_id=1, source_target_pairs={{16,112},{32,96},{48,80},{64,64},{80,48},{96,32},{112,16},{17,113}... | collective-permute-start | bytes 24584 | tf_op jit(solution)/shard_map/ppermute | solution.py:98
  364.3 13.3 %copy-start.5 = (f32[2]{0:T(128)S(1)}, f32[2]{0:T(128)}, u32[]{:S(2)}) copy-start(f32[2]{0:T(128)} %constant.79.clone) | copy-start | bytes 28
  412.1 17.3 %copy-start.4 = (s32[64]{0:T(128)S(1)}, s32[64]{0:T(128)}, u32[]{:S(2)}) copy-start(s32[64]{0:T(128)} %copy-done.3) | copy-start | bytes 772
  422.4 19.9 %all-to-all-start.4 = ((f32[8,1,32768]{2,1,0:T(1,128)}), f32[8,1,32768]{2,1,0:T(1,128)S(1)}, u32[]{:S(2)}, u32[]{:S(2)}) async-start(f32[8,1,32768]{2,1,0:T(1,128)} %reshape.738), calls=%async_computation.4 | async-start | bytes 2097152 | tf_op jit(solution)/shard_map/all_to_all | solution.py:91
  497.7 9.8 %copy-start.2 = (f32[32,8,4,32]{0,3,1,2:T(8,128)S(1)}, f32[32,8,4,32]{0,3,1,2:T(8,128)}, u32[]{:S(2)}) copy-start(f32[32,8,4,32]{0,3,1,2:T(8,128)} %get-tuple-element.12) | copy-start | bytes 393220
  497.7 10.4 %copy-start.1 = (f32[32,8,4,32]{0,3,1,2:T(8,128)S(1)}, f32[32,8,4,32]{0,3,1,2:T(8,128)}, u32[]{:S(2)}) copy-start(f32[32,8,4,32]{0,3,1,2:T(8,128)} %get-tuple-element.15) | copy-start | bytes 393220
  497.7 58.8 %all-to-all-start.5 = ((f32[16,1,65536]{2,1,0:T(1,128)}), f32[16,1,65536]{2,1,0:T(1,128)}, u32[]{:S(2)}, u32[]{:S(2)}) async-start(f32[16,1,65536]{2,1,0:T(1,128)} %reshape.740), calls=%async_computation.5 | async-start | bytes 8388608 | tf_op jit(solution)/shard_map/all_to_all | solution.py:92
